TPU v7x, 32 devices: a whole 2x2x4 slice. The times are simulated.
32 devices in a mesh: segment: 4 (over y, x), dp: 8 (over z, core).
Axes of the slice: x: 2, y: 2, z: 4, core: 2. Of those that a mesh axis runs over, the one named last changes fastest.
Arguments:
- images: bfloat16 [32, 16, 16, 512], P('dp'), may hold values from -6 to 6
- labels: int32 [32], P('dp'), may hold values from 0 to 999
- counts: int32 [4], replicated, may hold values from 1 to 4, as said below
- depthwise: bfloat16 [16, 9, 512], P('segment'), may hold values from -2 to 2
- pointwise: bfloat16 [16, 512, 512], P('segment'), may hold values from -0.09375 to 0.09375
- head_weight: float32 [512, 1000], replicated, may hold values from -0.25 to 0.25
Outputs:
- grad_pointwise: float32 [16, 512, 512], P('segment', 'dp')
- grad_depthwise: float32 [16, 9, 512], P('segment', None, 'dp')
Inputs may be any that keep to these rules, and one draw needn't show every extreme that they name: Section s runs its first counts[s] cell slots; some section runs all 4 and another a single cell.
All inputs are finite; a program needn't handle non-finite values.
Results may differ from a plain program's by a relative error of at most 0.00085.
Values may be sent and summed in bfloat16 or wider, within the bound.
A program may use at most 128 MiB of HBM per device.

v0:
```python
import functools

import jax
import jax.numpy as jnp
from jax import lax
from jax.experimental import pallas as pl
from jax.experimental.pallas import tpu as pltpu
from jax.sharding import PartitionSpec as P

LANES = 128
PAD = 2


def span(start, size):
    return pl.ds(pl.multiple_of(start, size), size)


def kernel(
    micros, slots, sections, side, image_total,
    images, target, depthwise, pointwise, pointwise_t, head_weight, live,
    grad_weight, grad_kernel,
    fields, spreads, cots, relu_pad, grad_pad, taps_acc, pooled,
    send_fwd, recv_fwd, send_bwd, recv_bwd,
):
    area = side * side
    width = images.shape[-1]
    here = lax.axis_index("segment")
    last = sections - 1
    chunks = [slice(c, c + LANES) for c in range(0, width, LANES)]

    def ahead(m):
        return pltpu.make_async_remote_copy(
            src_ref=fields.at[span((slots * micros + m) * area, area)],
            dst_ref=fields.at[span(m * area, area)],
            send_sem=send_fwd.at[m],
            recv_sem=recv_fwd.at[m],
            device_id={"segment": here + 1},
            device_id_type=pl.DeviceIdType.MESH,
        )

    def behind(m):
        return pltpu.make_async_remote_copy(
            src_ref=cots.at[span(m * area, area)],
            dst_ref=cots.at[span((slots * micros + m) * area, area)],
            send_sem=send_bwd.at[m],
            recv_sem=recv_bwd.at[m],
            device_id={"segment": here - 1},
            device_id_type=pl.DeviceIdType.MESH,
        )

    barrier = pltpu.get_barrier_semaphore()

    @pl.when(here > 0)
    def _():
        pl.semaphore_signal(
            barrier, inc=1, device_id={"segment": here - 1}, device_id_type=pl.DeviceIdType.MESH
        )

    @pl.when(here < last)
    def _():
        pl.semaphore_signal(
            barrier, inc=1, device_id={"segment": here + 1}, device_id_type=pl.DeviceIdType.MESH
        )

    inner_section = (here > 0) & (here < last)

    @pl.when(inner_section)
    def _():
        pl.semaphore_wait(barrier, 2)

    @pl.when(jnp.logical_not(inner_section))
    def _():
        pl.semaphore_wait(barrier, 1)

    edge = PAD * side
    for ref in (relu_pad, grad_pad.at[0], grad_pad.at[1], grad_pad.at[2]):
        ref[0:edge] = jnp.zeros((edge, width), jnp.float32)
        ref[edge + area : 2 * edge + area] = jnp.zeros((edge, width), jnp.float32)
    taps_acc[...] = jnp.zeros_like(taps_acc)
    cols = lax.broadcasted_iota(jnp.int32, (side, LANES), 0)

    def moved(value, shift):
        rolled = pltpu.roll(value, shift % side, 0)
        keep = cols >= shift if shift > 0 else cols < side + shift
        return jnp.where(keep, rolled, 0.0)

    def forward_cell(m, j, dilation):
        base = (j * micros + m) * area
        kernels = depthwise[j]
        relu_pad[edge : edge + area] = jnp.maximum(
            fields[span(base, area)].astype(jnp.float32), 0.0
        )
        for lanes in chunks:
            taps = [
                jnp.broadcast_to(kernels[t : t + 1, lanes], (side, LANES)) for t in range(9)
            ]

            def row_step(quad, carry):
                for extra in range(4):
                    row = quad * 4 + extra
                    rows = [
                        relu_pad[span((row + PAD + a * dilation) * side, side), lanes]
                        for a in (-1, 0, 1)
                    ]
                    parts = [
                        rows[0] * taps[b] + rows[1] * taps[3 + b] + rows[2] * taps[6 + b]
                        for b in range(3)
                    ]
                    total = parts[1] + moved(parts[0], dilation) + moved(parts[2], -dilation)
                    spreads[span(base + row * side, side), lanes] = total.astype(jnp.bfloat16)
                return carry

            lax.fori_loop(0, side // 4, row_step, 0)
        fields[span(base + micros * area, area)] = (
            fields[span(base, area)].astype(jnp.float32)
            + jnp.dot(
                spreads[span(base, area)], pointwise[j], preferred_element_type=jnp.float32
            )
        ).astype(jnp.bfloat16)

    def backward_cell(m, j, dilation):
        base = (j * micros + m) * area
        above = base + micros * area
        kernels = depthwise[j]
        grad_pad[1, edge : edge + area] = (
            jnp.dot(cots[span(above, area)], pointwise_t[j], preferred_element_type=jnp.float32)
            .astype(jnp.bfloat16)
            .astype(jnp.float32)
        )
        for lanes in chunks:
            taps = [
                jnp.broadcast_to(kernels[t : t + 1, lanes], (side, LANES)) for t in range(9)
            ]

            def shift_step(quad, carry):
                for extra in range(4):
                    at = span((quad * 4 + extra + PAD) * side, side)
                    value = grad_pad[1, at, lanes]
                    grad_pad[0, at, lanes] = moved(value, -dilation)
                    grad_pad[2, at, lanes] = moved(value, dilation)
                return carry

            lax.fori_loop(0, side // 4, shift_step, 0)

            def row_step(pair, sums):
                sums = list(sums)
                for extra in range(2):
                    row = pair * 2 + extra
                    field = fields[span(base + row * side, side), lanes].astype(jnp.float32)
                    relu = jnp.maximum(field, 0.0)
                    back = jnp.zeros((side, LANES), jnp.float32)
                    for t in range(9):
                        a, b = t // 3 - 1, t % 3
                        piece = grad_pad[
                            b, span((row + PAD - a * dilation) * side, side), lanes
                        ]
                        back = back + piece * taps[t]
                        term = piece * relu
                        sums[t] = sums[t] + (term[0:8] + term[8:16])
                    cot = cots[span(above + row * side, side), lanes].astype(jnp.float32)
                    cots[span(base + row * side, side), lanes] = (
                        cot + jnp.where(field > 0.0, back, 0.0)
                    ).astype(jnp.bfloat16)
                return tuple(sums)

            start = tuple(taps_acc[j, 8 * t : 8 * t + 8, lanes] for t in range(9))
            done = lax.fori_loop(0, side // 2, row_step, start)
            for t in range(9):
                taps_acc[j, 8 * t : 8 * t + 8, lanes] = done[t]

    def forward_micro(m, carry):
        @pl.when(here == 0)
        def _():
            fields[span(m * area, area)] = images[span(m * area, area)]

        @pl.when(here > 0)
        def _():
            ahead(m).wait_recv()

        def pair_step(pair, inner):
            for parity in range(2):
                forward_cell(m, pair * 2 + parity, 1 + parity)
            return inner

        lax.fori_loop(0, slots // 2, pair_step, 0)

        @pl.when(here < last)
        def _():
            ahead(m).start()

        return carry

    lax.fori_loop(0, micros, forward_micro, 0)

    @pl.when(here == last)
    def _():
        pooled[...] = jnp.zeros_like(pooled)
        for m in range(micros):
            final = fields[(slots * micros + m) * area : (slots * micros + m + 1) * area]
            pooled[m : m + 1] = jnp.sum(
                final.astype(jnp.float32), axis=0, keepdims=True
            ) * (1.0 / area)
        logits = jnp.dot(
            pooled[...],
            head_weight[...],
            precision=lax.Precision.HIGHEST,
            preferred_element_type=jnp.float32,
        )
        error_term = (1.0 / (1.0 + jnp.exp(-logits)) - target[...]) / image_total
        back = lax.dot_general(
            error_term,
            head_weight[...],
            (((1,), (1,)), ((), ())),
            precision=lax.Precision.HIGHEST,
            preferred_element_type=jnp.float32,
        ) / area
        for m in range(micros):
            cots[(slots * micros + m) * area : (slots * micros + m + 1) * area] = (
                jnp.broadcast_to(back[m : m + 1], (area, width)).astype(jnp.bfloat16)
            )

    def backward_micro(m, carry):
        @pl.when(here < last)
        def _():
            behind(m).wait_recv()

        def pair_step(pair, inner):
            for parity in (1, 0):
                backward_cell(m, slots - 2 - pair * 2 + parity, 1 + parity)
            return inner

        lax.fori_loop(0, slots // 2, pair_step, 0)

        @pl.when(here > 0)
        def _():
            behind(m).start()

        return carry

    lax.fori_loop(0, micros, backward_micro, 0)

    def finish(j, carry):
        rows = micros * area
        grad_weight[j] = (
            lax.dot_general(
                spreads[span(j * rows, rows)],
                cots[span((j + 1) * rows, rows)],
                (((0,), (0,)), ((), ())),
                preferred_element_type=jnp.float32,
            )
            * live[j, 0:1]
        )
        return carry

    lax.fori_loop(0, slots, finish, 0)
    for j in range(slots):
        for t in range(9):
            grad_kernel[j, t : t + 1] = jnp.sum(
                taps_acc[j, 8 * t : 8 * t + 8], axis=0, keepdims=True
            )

    @pl.when(here < last)
    def _():
        for m in range(micros):
            ahead(m).wait_send()

    @pl.when(here > 0)
    def _():
        for m in range(micros):
            behind(m).wait_send()


def local(images, labels, counts, depthwise, pointwise, head_weight):
    slots, _, width = depthwise.shape
    micros, side = images.shape[:2]
    area = side * side
    sections = lax.axis_size("segment")
    replicas = lax.axis_size("dp")
    here = lax.axis_index("segment")
    image_total = micros * replicas
    classes = head_weight.shape[1]
    classes_pad = -(-classes // LANES) * LANES
    count_here = jnp.sum(
        jnp.where(jnp.arange(sections, dtype=jnp.int32) == here, counts, 0)
    )
    live = jnp.arange(slots, dtype=jnp.int32) < count_here
    weight = jnp.where(live[:, None, None], pointwise, jnp.zeros((), pointwise.dtype))
    weight_t = jnp.swapaxes(weight, 1, 2)
    live_rows = jnp.broadcast_to(live.astype(jnp.float32)[:, None, None], (slots, 8, width))
    target = (labels[:, None] == jnp.arange(classes_pad, dtype=jnp.int32)[None, :]).astype(
        jnp.float32
    )
    target = jnp.pad(target, ((0, 8 - micros), (0, 0)))
    head = jnp.pad(head_weight, ((0, 0), (0, classes_pad - classes)))
    vmem = pl.BlockSpec(memory_space=pltpu.VMEM)
    padded = area + 2 * PAD * side
    grad_weight, grad_kernel = pl.pallas_call(
        functools.partial(kernel, micros, slots, sections, side, image_total),
        out_shape=(
            jax.ShapeDtypeStruct((slots, width, width), jnp.float32),
            jax.ShapeDtypeStruct((slots, 9, width), jnp.float32),
        ),
        in_specs=[vmem] * 7,
        out_specs=(vmem, vmem),
        scratch_shapes=[
            pltpu.VMEM(((slots + 1) * micros * area, width), jnp.bfloat16),
            pltpu.VMEM((slots * micros * area, width), jnp.bfloat16),
            pltpu.VMEM(((slots + 1) * micros * area, width), jnp.bfloat16),
            pltpu.VMEM((padded, width), jnp.float32),
            pltpu.VMEM((3, padded, width), jnp.float32),
            pltpu.VMEM((slots, 72, width), jnp.float32),
            pltpu.VMEM((8, width), jnp.float32),
            pltpu.SemaphoreType.DMA((micros,)),
            pltpu.SemaphoreType.DMA((micros,)),
            pltpu.SemaphoreType.DMA((micros,)),
            pltpu.SemaphoreType.DMA((micros,)),
        ],
        compiler_params=pltpu.CompilerParams(
            collective_id=0, has_side_effects=True, vmem_limit_bytes=52 * 1024 * 1024
        ),
    )(
        images.reshape(micros * area, width),
        target,
        depthwise.astype(jnp.float32),
        weight,
        weight_t,
        head,
        live_rows,
    )
    part = width // replicas
    rest = grad_kernel.reshape(slots, 9, replicas, part).swapaxes(1, 2)
    rest = rest.reshape(slots, replicas, 9 * part)
    rest = jnp.pad(rest, ((0, 0), (0, 0), (0, 8 * width - 9 * part)))
    rest = rest.reshape(slots, replicas, 8, width)
    packed = jnp.concatenate([grad_weight.reshape(slots, replicas, part, width), rest], axis=2)
    packed = packed.reshape(slots, replicas * (part + 8), width)
    summed = lax.psum_scatter(packed, "dp", scatter_dimension=1, tiled=True)
    return (
        summed[:, :part],
        summed[:, part:].reshape(slots, 8 * width)[:, : 9 * part].reshape(slots, 9, part),
    )


def solution(mesh):
    in_specs = (
        P("dp", None, None, None),
        P("dp"),
        P(),
        P("segment", None, None),
        P("segment", None, None),
        P(),
    )
    out_specs = (P("segment", "dp", None), P("segment", None, "dp"))
    return jax.shard_map(local, mesh=mesh, in_specs=in_specs, out_specs=out_specs, check_vma=False)
```

profile of v0, /device:TPU:0, one launch (start us, length us, event | category | flops | bytes accessed | tf_op | source)
XLA Modules:
  0.0 219.8 jit_solution(4957107745986783985)
XLA Ops:
  7.2 0.0 reduce-scatter.2.cloned.1.call-start
  7.2 1.3 fusion
  8.5 0.6 iota_compare_fusion.1
  9.2 2.8 %copy.13 = bf16[4,512,512]{1,2,0:T(8,128)(2,1)S(1)} copy(bf16[4,512,512]{2,1,0:T(8,128)(2,1)} %param.10) | data formatting | bytes 4194304 | tf_op args[4]
  12.0 1.5 fusion.2.pointwise_t
  13.5 1.5 broadcast_select_fusion
  15.0 0.1 iota_compare_fusion
  15.2 4.1 %copy.15.pointwise = bf16[4,512,512]{2,1,0:T(8,128)(2,1)} copy(bf16[4,512,512]{1,2,0:T(8,128)(2,1)} %broadcast_select_fusion) | data formatting | bytes 4194304 | tf_op jit(solution)/shard_map/jit(_where)/select_n | solution.py:287
  19.3 1.9 copy.14
  21.2 1.5 pad.16.head_weight
  22.7 0.1 broadcast_in_dim.28.live
  22.8 126.3 %shard_map.77 = (f32[4,512,512]{2,1,0:T(8,128)}, f32[4,9,512]{2,1,0:T(8,128)S(1)}) custom-call(bf16[1024,512]{1,0:T(8,128)(2,1)S(1)} %bitcast.12, f32[8,1024]{1,0:T(8,128)S(1)} %pad_convert_fusion.target, f32[4,9,512]{2,1,0:T(8,128)S(1)} %copy_convert_fusion.depthwise, bf16[4,512,512]{2,1,0:T(8,128)(2,1)} %copy.15.pointwise, ...), custom_call_target="tpu_custom_call" | custom-call | tf_op jit(solution)/shard_map/pallas_call | solution.py:297
  149.2 0.1 copy.16
  149.2 0.1 reshape.38
  149.3 0.1 copy.17
  149.4 0.1 reshape.39
  149.6 0.3 copy.18
  149.9 5.1 %pad_maximum_fusion = f32[4,8,72,512]{3,2,1,0:T(8,128)} fusion(f32[4,8,8,512]{3,2,1,0:T(8,128)S(1)} %copy.18, f32[4,8,64,512]{3,2,1,0:T(8,128)} %bitcast.14), kind=kLoop, calls=%fused_computation | loop fusion | flops 1179648 | bytes 9437184 | tf_op jit(solution)/shard_map/concatenate | solution.py:335
  155.0 0.0 reduce-scatter.2.cloned.1.call-update
  155.0 54.5 %reduce-scatter.2.cloned.1.call-done = f32[4,72,512]{2,1,0:T(8,128)} async-done(((f32[4,576,512]{2,1,0:T(8,128)}), f32[4,72,512]{2,1,0:T(8,128)}) %reduce-scatter.2.cloned.1.call-update) | async-done | bytes 589840 | tf_op jit(solution)/shard_map/reduce_scatter | solution.py:337
  209.5 0.8 slice_bitcast_fusion
  210.4 0.1 reshape.43
  210.5 0.6 copy.19
  211.1 1.9 slice.12
  (11 shorter events, 0.1 us)
Async XLA Ops:
  7.2 202.3 %reduce-scatter.2.cloned.1.call-start = ((), (), s32[]{:S(2)}) async-start(), calls=%async_computation.1 | async-start | bytes 5308416 | tf_op jit(solution)/shard_map/reduce_scatter | solution.py:337
  13.5 1.5 copy-start.2
  13.5 1.6 copy-start.1
  21.2 1.6 copy-start
Sparse Core Ops, SparseCore 0:
  155.1 54.3 reduce-scatter.1
where the time goes:
time: 220 us
  Pallas kernels  126 us (57%)
  waiting for transfers between devices  54.5 us (25%)
  local copies, waits for them, and re-layouts  14.6 us (7%)
  between operations  14.1 us (6%)
  other arithmetic  10.2 us (5%)
    pallas_call x1, Pallas kernels, local(): pl.pallas_call(functools.partial(kernel, micros, slots, sections, side, i...  126 us
    reduce_scatter x1, waiting for transfers between devices, local(): summed = lax.psum_scatter(packed, 'dp', scatter_dimension=1, tiled=True)  54.5 us
    unnamed x11, local copies, waits for them, and re-layouts  6.22 us
    concatenate x1, other arithmetic, local(): jnp.concatenate([grad_weight.reshape(slots, replicas, part, width), rest]...  5.09 us
  transfers between devices with their start and end apart: 1, of which 1 were waited for; matrix products, arithmetic and copies ran while one was open for 0% of the time, Pallas kernels for 0%

commit v1 on v0

--- a/solution.py
+++ b/solution.py
@@ -16,11 +16,13 @@
 
 
 def kernel(
-    micros, slots, sections, side, image_total,
-    images, target, depthwise, pointwise, pointwise_t, head_weight, live,
+    micros, slots, sections, chips, side, image_total,
+    labels, counts, images, depthwise, pointwise, head_weight,
     grad_weight, grad_kernel,
-    fields, spreads, cots, relu_pad, grad_pad, taps_acc, pooled,
+    fields, spreads, cots, relu_pad, grad_pad, taps_acc, pooled, pointwise_t,
+    whole, twin, rise, fall, whole_k, twin_k, rise_k, fall_k,
     send_fwd, recv_fwd, send_bwd, recv_bwd,
+    send_twin, recv_twin, send_rise, recv_rise, send_fall, recv_fall,
 ):
     area = side * side
     width = images.shape[-1]
@@ -48,29 +50,67 @@
             device_id_type=pl.DeviceIdType.MESH,
         )
 
+    replica = lax.axis_index("dp")
+    chip, core = lax.div(replica, 2), lax.rem(replica, 2)
+    part = grad_weight.shape[1]
+
+    def to_twin(j):
+        if j is None:
+            src, dst, at = whole_k, twin_k, slots
+        else:
+            src, dst, at = whole.at[j, :, 1 - core], twin.at[j], j
+        return pltpu.make_async_remote_copy(
+            src_ref=src, dst_ref=dst, send_sem=send_twin.at[at], recv_sem=recv_twin.at[at],
+            device_id={"dp": replica + 1 - 2 * core}, device_id_type=pl.DeviceIdType.MESH,
+        )
+
+    def up(j, k):
+        ref, at = (rise_k.at[k], slots) if j is None else (rise.at[j, k], j)
+        return pltpu.make_async_remote_copy(
+            src_ref=ref, dst_ref=ref, send_sem=send_rise.at[at, k], recv_sem=recv_rise.at[at, k],
+            device_id={"dp": replica + 2}, device_id_type=pl.DeviceIdType.MESH,
+        )
+
+    def down(j, k):
+        ref, at = (fall_k.at[k], slots) if j is None else (fall.at[j, k], j)
+        return pltpu.make_async_remote_copy(
+            src_ref=ref, dst_ref=ref, send_sem=send_fall.at[at, k], recv_sem=recv_fall.at[at, k],
+            device_id={"dp": replica - 2}, device_id_type=pl.DeviceIdType.MESH,
+        )
+
+    def own(j, k):
+        if j is None:
+            return whole_k[k] + twin_k[k]
+        return whole[j, k, core] + twin[j, k]
+
     barrier = pltpu.get_barrier_semaphore()
 
-    @pl.when(here > 0)
-    def _():
-        pl.semaphore_signal(
-            barrier, inc=1, device_id={"segment": here - 1}, device_id_type=pl.DeviceIdType.MESH
-        )
-
-    @pl.when(here < last)
-    def _():
-        pl.semaphore_signal(
-            barrier, inc=1, device_id={"segment": here + 1}, device_id_type=pl.DeviceIdType.MESH
-        )
-
-    inner_section = (here > 0) & (here < last)
-
-    @pl.when(inner_section)
-    def _():
-        pl.semaphore_wait(barrier, 2)
-
-    @pl.when(jnp.logical_not(inner_section))
-    def _():
-        pl.semaphore_wait(barrier, 1)
+    def greet(where, target):
+        @pl.when(where)
+        def _():
+            pl.semaphore_signal(
+                barrier, inc=1, device_id=target, device_id_type=pl.DeviceIdType.MESH
+            )
+
+        return jnp.where(where, 1, 0).astype(jnp.int32)
+
+    peers = greet(here > 0, {"segment": here - 1})
+    peers += greet(here < last, {"segment": here + 1})
+    peers += greet(chip > 0, {"dp": replica - 2})
+    peers += greet(chip < chips - 1, {"dp": replica + 2})
+    pl.semaphore_signal(
+        barrier, inc=1, device_id={"dp": replica + 1 - 2 * core},
+        device_id_type=pl.DeviceIdType.MESH,
+    )
+    pl.semaphore_wait(barrier, peers + 1)
+    count_here = counts[here]
+
+    def live(j):
+        return jnp.where(j < count_here, 1.0, 0.0)
+
+    def turn_weights():
+        for j in range(slots):
+            pointwise_t[j] = jnp.swapaxes(pointwise[j], 0, 1)
 
     edge = PAD * side
     for ref in (relu_pad, grad_pad.at[0], grad_pad.at[1], grad_pad.at[2]):
@@ -86,7 +126,7 @@
 
     def forward_cell(m, j, dilation):
         base = (j * micros + m) * area
-        kernels = depthwise[j]
+        kernels = depthwise[j].astype(jnp.float32)
         relu_pad[edge : edge + area] = jnp.maximum(
             fields[span(base, area)].astype(jnp.float32), 0.0
         )
@@ -116,14 +156,20 @@
             + jnp.dot(
                 spreads[span(base, area)], pointwise[j], preferred_element_type=jnp.float32
             )
+            * live(j)
         ).astype(jnp.bfloat16)
 
     def backward_cell(m, j, dilation):
         base = (j * micros + m) * area
         above = base + micros * area
-        kernels = depthwise[j]
+        kernels = depthwise[j].astype(jnp.float32)
         grad_pad[1, edge : edge + area] = (
-            jnp.dot(cots[span(above, area)], pointwise_t[j], preferred_element_type=jnp.float32)
+            (
+                jnp.dot(
+                    cots[span(above, area)], pointwise_t[j], preferred_element_type=jnp.float32
+                )
+                * live(j)
+            )
             .astype(jnp.bfloat16)
             .astype(jnp.float32)
         )
@@ -171,7 +217,7 @@
     def forward_micro(m, carry):
         @pl.when(here == 0)
         def _():
-            fields[span(m * area, area)] = images[span(m * area, area)]
+            fields[span(m * area, area)] = images[m].reshape(area, width)
 
         @pl.when(here > 0)
         def _():
@@ -190,7 +236,9 @@
 
         return carry
 
+    pl.when(here == last)(turn_weights)
     lax.fori_loop(0, micros, forward_micro, 0)
+    pl.when(here < last)(turn_weights)
 
     @pl.when(here == last)
     def _():
@@ -206,7 +254,12 @@
             precision=lax.Precision.HIGHEST,
             preferred_element_type=jnp.float32,
         )
-        error_term = (1.0 / (1.0 + jnp.exp(-logits)) - target[...]) / image_total
+        classes = lax.broadcasted_iota(jnp.int32, logits.shape, 1)
+        image = lax.broadcasted_iota(jnp.int32, logits.shape, 0)
+        target = jnp.zeros(logits.shape, jnp.float32)
+        for m in range(micros):
+            target += jnp.where((image == m) & (classes == labels[m]), 1.0, 0.0)
+        error_term = (1.0 / (1.0 + jnp.exp(-logits)) - target) / image_total
         back = lax.dot_general(
             error_term,
             head_weight[...],
@@ -241,23 +294,103 @@
 
     def finish(j, carry):
         rows = micros * area
-        grad_weight[j] = (
+        total = (
             lax.dot_general(
                 spreads[span(j * rows, rows)],
                 cots[span((j + 1) * rows, rows)],
                 (((0,), (0,)), ((), ())),
                 preferred_element_type=jnp.float32,
             )
-            * live[j, 0:1]
-        )
+            * live(j)
+        )
+        whole[j] = total.reshape(chips, 2, part, width)
+        to_twin(j).start()
         return carry
 
     lax.fori_loop(0, slots, finish, 0)
+    whole_k[...] = jnp.zeros_like(whole_k)
     for j in range(slots):
         for t in range(9):
-            grad_kernel[j, t : t + 1] = jnp.sum(
-                taps_acc[j, 8 * t : 8 * t + 8], axis=0, keepdims=True
-            )
+            tap_sum = jnp.sum(taps_acc[j, 8 * t : 8 * t + 8], axis=0, keepdims=True)
+            for k in range(chips):
+                lane = 2 * part * k // LANES * LANES
+                whole_k[k, 16 * j + t : 16 * j + t + 1] = tap_sum[:, lane : lane + LANES]
+    to_twin(None).start()
+
+    def relay(j):
+        rising, falling = (rise_k, fall_k) if j is None else (rise.at[j], fall.at[j])
+
+        def block_step(i, carry):
+            k_up, k_down = chips - 1 - i, i
+
+            @pl.when(k_up > chip)
+            def _():
+                @pl.when(chip == 0)
+                def _():
+                    rising[k_up] = own(j, k_up)
+
+                @pl.when(chip > 0)
+                def _():
+                    up(j, k_up).wait_recv()
+                    rising[k_up] = rising[k_up] + own(j, k_up)
+
+                up(j, k_up).start()
+
+            @pl.when(k_down < chip)
+            def _():
+                @pl.when(chip == chips - 1)
+                def _():
+                    falling[k_down] = own(j, k_down)
+
+                @pl.when(chip < chips - 1)
+                def _():
+                    down(j, k_down).wait_recv()
+                    falling[k_down] = falling[k_down] + own(j, k_down)
+
+                down(j, k_down).start()
+
+            return carry
+
+        to_twin(j).wait_recv()
+        lax.fori_loop(0, chips - 1, block_step, 0)
+
+    def settle(j):
+        rising, falling = (rise_k, fall_k) if j is None else (rise.at[j], fall.at[j])
+        out = grad_kernel if j is None else grad_weight.at[j]
+        out[...] = own(j, chip)
+
+        @pl.when(chip > 0)
+        def _():
+            up(j, chip).wait_recv()
+            out[...] = out[...] + rising[chip]
+
+        @pl.when(chip < chips - 1)
+        def _():
+            down(j, chip).wait_recv()
+            out[...] = out[...] + falling[chip]
+
+    def sent(j):
+        def block_step(k, carry):
+            @pl.when(k > chip)
+            def _():
+                up(j, k).wait_send()
+
+            @pl.when(k < chip)
+            def _():
+                down(j, k).wait_send()
+
+            return carry
+
+        to_twin(j).wait_send()
+        lax.fori_loop(0, chips, block_step, 0)
+
+    for step in (relay, settle, sent):
+        def slot_step(j, carry, step=step):
+            step(j)
+            return carry
+
+        lax.fori_loop(0, slots, slot_step, 0)
+        step(None)
 
     @pl.when(here < last)
     def _():
@@ -276,31 +409,20 @@
     area = side * side
     sections = lax.axis_size("segment")
     replicas = lax.axis_size("dp")
-    here = lax.axis_index("segment")
-    image_total = micros * replicas
-    classes = head_weight.shape[1]
-    classes_pad = -(-classes // LANES) * LANES
-    count_here = jnp.sum(
-        jnp.where(jnp.arange(sections, dtype=jnp.int32) == here, counts, 0)
-    )
-    live = jnp.arange(slots, dtype=jnp.int32) < count_here
-    weight = jnp.where(live[:, None, None], pointwise, jnp.zeros((), pointwise.dtype))
-    weight_t = jnp.swapaxes(weight, 1, 2)
-    live_rows = jnp.broadcast_to(live.astype(jnp.float32)[:, None, None], (slots, 8, width))
-    target = (labels[:, None] == jnp.arange(classes_pad, dtype=jnp.int32)[None, :]).astype(
-        jnp.float32
-    )
-    target = jnp.pad(target, ((0, 8 - micros), (0, 0)))
-    head = jnp.pad(head_weight, ((0, 0), (0, classes_pad - classes)))
+    chips = replicas // 2
+    part = width // replicas
     vmem = pl.BlockSpec(memory_space=pltpu.VMEM)
+    smem = pl.BlockSpec(memory_space=pltpu.SMEM)
     padded = area + 2 * PAD * side
+    blocks = pltpu.VMEM((slots, chips, part, width), jnp.float32)
+    blocks_k = pltpu.VMEM((chips, slots * 16, LANES), jnp.float32)
     grad_weight, grad_kernel = pl.pallas_call(
-        functools.partial(kernel, micros, slots, sections, side, image_total),
+        functools.partial(kernel, micros, slots, sections, chips, side, micros * replicas),
         out_shape=(
-            jax.ShapeDtypeStruct((slots, width, width), jnp.float32),
-            jax.ShapeDtypeStruct((slots, 9, width), jnp.float32),
+            jax.ShapeDtypeStruct((slots, part, width), jnp.float32),
+            jax.ShapeDtypeStruct((slots * 16, LANES), jnp.float32),
         ),
-        in_specs=[vmem] * 7,
+        in_specs=[smem] * 2 + [vmem] * 4,
         out_specs=(vmem, vmem),
         scratch_shapes=[
             pltpu.VMEM(((slots + 1) * micros * area, width), jnp.bfloat16),
@@ -310,35 +432,21 @@
             pltpu.VMEM((3, padded, width), jnp.float32),
             pltpu.VMEM((slots, 72, width), jnp.float32),
             pltpu.VMEM((8, width), jnp.float32),
-            pltpu.SemaphoreType.DMA((micros,)),
-            pltpu.SemaphoreType.DMA((micros,)),
-            pltpu.SemaphoreType.DMA((micros,)),
-            pltpu.SemaphoreType.DMA((micros,)),
-        ],
+            pltpu.VMEM((slots, width, width), jnp.bfloat16),
+            pltpu.VMEM((slots, chips, 2, part, width), jnp.float32),
+            blocks, blocks, blocks,
+            blocks_k, blocks_k, blocks_k, blocks_k,
+        ]
+        + [pltpu.SemaphoreType.DMA((micros,))] * 4
+        + [pltpu.SemaphoreType.DMA((slots + 1,))] * 2
+        + [pltpu.SemaphoreType.DMA((slots + 1, chips))] * 4,
         compiler_params=pltpu.CompilerParams(
-            collective_id=0, has_side_effects=True, vmem_limit_bytes=52 * 1024 * 1024
+            collective_id=0, has_side_effects=True, vmem_limit_bytes=56 * 1024 * 1024
         ),
-    )(
-        images.reshape(micros * area, width),
-        target,
-        depthwise.astype(jnp.float32),
-        weight,
-        weight_t,
-        head,
-        live_rows,
-    )
-    part = width // replicas
-    rest = grad_kernel.reshape(slots, 9, replicas, part).swapaxes(1, 2)
-    rest = rest.reshape(slots, replicas, 9 * part)
-    rest = jnp.pad(rest, ((0, 0), (0, 0), (0, 8 * width - 9 * part)))
-    rest = rest.reshape(slots, replicas, 8, width)
-    packed = jnp.concatenate([grad_weight.reshape(slots, replicas, part, width), rest], axis=2)
-    packed = packed.reshape(slots, replicas * (part + 8), width)
-    summed = lax.psum_scatter(packed, "dp", scatter_dimension=1, tiled=True)
-    return (
-        summed[:, :part],
-        summed[:, part:].reshape(slots, 8 * width)[:, : 9 * part].reshape(slots, 9, part),
-    )
+    )(labels, counts, images, depthwise, pointwise, head_weight)
+    lane = lax.rem(lax.axis_index("dp") * part, LANES)
+    mine = lax.dynamic_slice_in_dim(grad_kernel, lane, part, 1)
+    return grad_weight, mine.reshape(slots, 16, part)[:, :9]
 
 
 def solution(mesh):

time: 220 us -> 188 us (0.85)
  waiting for transfers between devices: 54.5 us -> 0 us
  Pallas kernels: 126 us -> 179 us
  between operations: 14.1 us -> 0.65 us
  other arithmetic: 10.2 us -> 0 us
  local copies, waits for them, and re-layouts: 14.6 us -> 7.66 us
    reduce_scatter x1 -> x0, waiting for transfers between devices: 54.5 us -> none  [local(): summed = lax.psum_scatter(packed, 'dp', scatter_dimension=1, tiled=True)]
    pallas_call x1, Pallas kernels: 126 us -> 179 us  [local(): pl.pallas_call(functools.partial(kernel, micros, slots, sections, chips,...]
    concatenate x1 -> x0, other arithmetic: 5.09 us -> none  [local(): jnp.concatenate([grad_weight.reshape(slots, replicas, part, width), rest]...]
    select_n x1 -> x0, local copies, waits for them, and re-layouts: 4.13 us -> none  [local(): jnp.where(live[:, None, None], pointwise, jnp.zeros((), pointwise.dtype))]
    unnamed x11 -> x4, local copies, waits for them, and re-layouts: 6.22 us -> 6.83 us
  transfers between devices with their start and end apart: 1 -> 0, of which waited for: 1 -> 0; matrix products, arithmetic and copies ran while one was open for 0% -> 0% of each run, Pallas kernels for 0% -> 0%
where the time goes in v1:
time: 188 us; the launch traced here: 187 us
  Pallas kernels  179 us (95%)
  local copies, waits for them, and re-layouts  7.66 us (4%)
    pallas_call x1, Pallas kernels, local(): pl.pallas_call(functools.partial(kernel, micros, slots, sections, chips,...  179 us
    unnamed x4, local copies, waits for them, and re-layouts  6.83 us

profile of v1, /device:TPU:0, one launch (start us, length us, event | category | flops | bytes accessed | tf_op | source)
XLA Modules:
  0.0 187.2 jit_solution(17681953404750761581)
XLA Ops:
  0.6 1.4 copy.10.depthwise
  2.0 2.9 %copy.11.head_weight = f32[512,1000]{1,0:T(8,128)} copy(f32[512,1000]{0,1:T(8,128)} %param.11) | data formatting | bytes 4096000 | tf_op args[5]
  5.0 178.9 %shard_map.77 = (f32[4,64,512]{2,1,0:T(8,128)}, f32[64,128]{1,0:T(8,128)}) custom-call(s32[4]{0:T(128)} %labels.1, s32[4]{0:T(128)} %counts.1, bf16[4,16,16,512]{3,2,1,0:T(8,128)(2,1)} %images.1, bf16[4,9,512]{2,1,0:T(8,128)(2,1)} %copy.10.depthwise, bf16[4,512,512]{2,1,0:T(8,128)(2,1)} %pointwise.1, f32[512,1000]{1,0:T(8,128)} %copy.11.head_weight), custom_call_target="tpu_custom_call" | custom-call | tf_op jit(solution)/shard_map/pallas_call | solution.py:419
  183.9 0.8 constant_dynamic-slice_fusion
  184.7 0.6 copy.12
  185.3 1.9 copy.14

commit v2 on v1

--- a/solution.py
+++ b/solution.py
@@ -19,7 +19,7 @@
     micros, slots, sections, chips, side, image_total,
     labels, counts, images, depthwise, pointwise, head_weight,
     grad_weight, grad_kernel,
-    fields, spreads, cots, relu_pad, grad_pad, taps_acc, pooled, pointwise_t,
+    fields, spreads, cots, relu_pad, grad_pad, taps_acc, pooled, pointwise_t, tap_rows,
     whole, twin, rise, fall, whole_k, twin_k, rise_k, fall_k,
     send_fwd, recv_fwd, send_bwd, recv_bwd,
     send_twin, recv_twin, send_rise, recv_rise, send_fall, recv_fall,
@@ -117,6 +117,10 @@
         ref[0:edge] = jnp.zeros((edge, width), jnp.float32)
         ref[edge + area : 2 * edge + area] = jnp.zeros((edge, width), jnp.float32)
     taps_acc[...] = jnp.zeros_like(taps_acc)
+    for t in range(9):
+        tap_values = depthwise[t].astype(jnp.float32)
+        for j in range(slots):
+            tap_rows[j, t : t + 1] = tap_values[j : j + 1]
     cols = lax.broadcasted_iota(jnp.int32, (side, LANES), 0)
 
     def moved(value, shift):
@@ -126,7 +130,7 @@
 
     def forward_cell(m, j, dilation):
         base = (j * micros + m) * area
-        kernels = depthwise[j].astype(jnp.float32)
+        kernels = tap_rows[j]
         relu_pad[edge : edge + area] = jnp.maximum(
             fields[span(base, area)].astype(jnp.float32), 0.0
         )
@@ -162,7 +166,7 @@
     def backward_cell(m, j, dilation):
         base = (j * micros + m) * area
         above = base + micros * area
-        kernels = depthwise[j].astype(jnp.float32)
+        kernels = tap_rows[j]
         grad_pad[1, edge : edge + area] = (
             (
                 jnp.dot(
@@ -248,9 +252,10 @@
             pooled[m : m + 1] = jnp.sum(
                 final.astype(jnp.float32), axis=0, keepdims=True
             ) * (1.0 / area)
-        logits = jnp.dot(
+        logits = lax.dot_general(
             pooled[...],
             head_weight[...],
+            (((1,), (1,)), ((), ())),
             precision=lax.Precision.HIGHEST,
             preferred_element_type=jnp.float32,
         )
@@ -260,10 +265,9 @@
         for m in range(micros):
             target += jnp.where((image == m) & (classes == labels[m]), 1.0, 0.0)
         error_term = (1.0 / (1.0 + jnp.exp(-logits)) - target) / image_total
-        back = lax.dot_general(
+        back = jnp.dot(
             error_term,
             head_weight[...],
-            (((1,), (1,)), ((), ())),
             precision=lax.Precision.HIGHEST,
             preferred_element_type=jnp.float32,
         ) / area
@@ -272,27 +276,26 @@
                 jnp.broadcast_to(back[m : m + 1], (area, width)).astype(jnp.bfloat16)
             )
 
-    def backward_micro(m, carry):
-        @pl.when(here < last)
-        def _():
-            behind(m).wait_recv()
-
-        def pair_step(pair, inner):
-            for parity in (1, 0):
-                backward_cell(m, slots - 2 - pair * 2 + parity, 1 + parity)
-            return inner
-
-        lax.fori_loop(0, slots // 2, pair_step, 0)
-
-        @pl.when(here > 0)
-        def _():
-            behind(m).start()
-
-        return carry
-
-    lax.fori_loop(0, micros, backward_micro, 0)
-
-    def finish(j, carry):
+    def launch(j):
+        rising, falling = (rise_k, fall_k) if j is None else (rise.at[j], fall.at[j])
+
+        def block_step(i, carry):
+            @pl.when(chip == 0)
+            def _():
+                rising[chips - 1 - i] = own(j, chips - 1 - i)
+                up(j, chips - 1 - i).start()
+
+            @pl.when(chip == chips - 1)
+            def _():
+                falling[i] = own(j, i)
+                down(j, i).start()
+
+            return carry
+
+        to_twin(j).wait_recv()
+        lax.fori_loop(0, chips - 1, block_step, 0)
+
+    def finish(j):
         rows = micros * area
         total = (
             lax.dot_general(
@@ -305,9 +308,46 @@
         )
         whole[j] = total.reshape(chips, 2, part, width)
         to_twin(j).start()
+
+        @pl.when(j < slots - 1)
+        def _():
+            launch(j + 1)
+
+    def backward_micro(m, carry):
+        @pl.when(here < last)
+        def _():
+            behind(m).wait_recv()
+
+        def pair_step(pair, inner):
+            for parity in (1, 0):
+                slot = slots - 2 - pair * 2 + parity
+                backward_cell(m, slot, 1 + parity)
+
+                @pl.when((m == micros - 1) & (here == 0))
+                def _(slot=slot):
+                    finish(slot)
+
+            return inner
+
+        lax.fori_loop(0, slots // 2, pair_step, 0)
+
+        @pl.when(here > 0)
+        def _():
+            behind(m).start()
+
         return carry
 
-    lax.fori_loop(0, slots, finish, 0)
+    lax.fori_loop(0, micros, backward_micro, 0)
+
+    @pl.when(here > 0)
+    def _():
+        def slot_step(i, carry):
+            finish(slots - 1 - i)
+            return carry
+
+        lax.fori_loop(0, slots, slot_step, 0)
+
+    launch(0)
     whole_k[...] = jnp.zeros_like(whole_k)
     for j in range(slots):
         for t in range(9):
@@ -316,6 +356,7 @@
                 lane = 2 * part * k // LANES * LANES
                 whole_k[k, 16 * j + t : 16 * j + t + 1] = tap_sum[:, lane : lane + LANES]
     to_twin(None).start()
+    launch(None)
 
     def relay(j):
         rising, falling = (rise_k, fall_k) if j is None else (rise.at[j], fall.at[j])
@@ -323,35 +364,20 @@
         def block_step(i, carry):
             k_up, k_down = chips - 1 - i, i
 
-            @pl.when(k_up > chip)
-            def _():
-                @pl.when(chip == 0)
-                def _():
-                    rising[k_up] = own(j, k_up)
-
-                @pl.when(chip > 0)
-                def _():
-                    up(j, k_up).wait_recv()
-                    rising[k_up] = rising[k_up] + own(j, k_up)
-
+            @pl.when((k_up > chip) & (chip > 0))
+            def _():
+                up(j, k_up).wait_recv()
+                rising[k_up] = rising[k_up] + own(j, k_up)
                 up(j, k_up).start()
 
-            @pl.when(k_down < chip)
-            def _():
-                @pl.when(chip == chips - 1)
-                def _():
-                    falling[k_down] = own(j, k_down)
-
-                @pl.when(chip < chips - 1)
-                def _():
-                    down(j, k_down).wait_recv()
-                    falling[k_down] = falling[k_down] + own(j, k_down)
-
+            @pl.when((k_down < chip) & (chip < chips - 1))
+            def _():
+                down(j, k_down).wait_recv()
+                falling[k_down] = falling[k_down] + own(j, k_down)
                 down(j, k_down).start()
 
             return carry
 
-        to_twin(j).wait_recv()
         lax.fori_loop(0, chips - 1, block_step, 0)
 
     def settle(j):
@@ -386,7 +412,7 @@
 
     for step in (relay, settle, sent):
         def slot_step(j, carry, step=step):
-            step(j)
+            step(slots - 1 - j)
             return carry
 
         lax.fori_loop(0, slots, slot_step, 0)
@@ -433,6 +459,7 @@
             pltpu.VMEM((slots, 72, width), jnp.float32),
             pltpu.VMEM((8, width), jnp.float32),
             pltpu.VMEM((slots, width, width), jnp.bfloat16),
+            pltpu.VMEM((slots, 16, width), jnp.float32),
             pltpu.VMEM((slots, chips, 2, part, width), jnp.float32),
             blocks, blocks, blocks,
             blocks_k, blocks_k, blocks_k, blocks_k,
@@ -443,7 +470,7 @@
         compiler_params=pltpu.CompilerParams(
             collective_id=0, has_side_effects=True, vmem_limit_bytes=56 * 1024 * 1024
         ),
-    )(labels, counts, images, depthwise, pointwise, head_weight)
+    )(labels, counts, images, jnp.swapaxes(depthwise, 0, 1), pointwise, head_weight.T)
     lane = lax.rem(lax.axis_index("dp") * part, LANES)
     mine = lax.dynamic_slice_in_dim(grad_kernel, lane, part, 1)
     return grad_weight, mine.reshape(slots, 16, part)[:, :9]

time: 188 us -> 182 us (0.968)
  local copies, waits for them, and re-layouts: 7.66 us -> 3.33 us
    unnamed x4 -> x2, local copies, waits for them, and re-layouts: 6.83 us -> 2.49 us
where the time goes in v2:
time: 182 us
  Pallas kernels  178 us (98%)
  local copies, waits for them, and re-layouts  3.33 us (2%)
    pallas_call x1, Pallas kernels, local(): pl.pallas_call(functools.partial(kernel, micros, slots, sections, chips,...  178 us

profile of v2, /device:TPU:0, one launch (start us, length us, event | category | flops | bytes accessed | tf_op | source)
XLA Modules:
  0.0 181.8 jit_solution(14095565207645701164)
XLA Ops:
  0.6 177.8 %shard_map.77 = (f32[4,64,512]{2,1,0:T(8,128)}, f32[64,128]{1,0:T(8,128)}) custom-call(s32[4]{0:T(128)} %labels.1, s32[4]{0:T(128)} %counts.1, bf16[4,16,16,512]{3,2,1,0:T(8,128)(2,1)} %images.1, bf16[9,4,512]{2,1,0:T(4,128)(2,1)} %bitcast.6, bf16[4,512,512]{2,1,0:T(8,128)(2,1)} %pointwise.1, f32[1000,512]{1,0:T(8,128)} %bitcast.4), custom_call_target="tpu_custom_call" | custom-call | tf_op jit(solution)/shard_map/pallas_call | solution.py:445
  178.5 0.8 constant_dynamic-slice_fusion
  179.3 0.6 copy.8
  179.9 1.9 %copy.10 = f32[4,64,512]{2,1,0:T(8,128)} copy(f32[4,64,512]{2,1,0:T(8,128)} %get-tuple-element.10) | data formatting | bytes 1048576

commit v3 on v2

--- a/solution.py
+++ b/solution.py
@@ -140,8 +140,8 @@
             ]
 
             def row_step(quad, carry):
-                for extra in range(4):
-                    row = quad * 4 + extra
+                for extra in range(8):
+                    row = quad * 8 + extra
                     rows = [
                         relu_pad[span((row + PAD + a * dilation) * side, side), lanes]
                         for a in (-1, 0, 1)
@@ -154,7 +154,7 @@
                     spreads[span(base + row * side, side), lanes] = total.astype(jnp.bfloat16)
                 return carry
 
-            lax.fori_loop(0, side // 4, row_step, 0)
+            lax.fori_loop(0, side // 8, row_step, 0)
         fields[span(base + micros * area, area)] = (
             fields[span(base, area)].astype(jnp.float32)
             + jnp.dot(
@@ -183,19 +183,19 @@
             ]
 
             def shift_step(quad, carry):
-                for extra in range(4):
-                    at = span((quad * 4 + extra + PAD) * side, side)
+                for extra in range(8):
+                    at = span((quad * 8 + extra + PAD) * side, side)
                     value = grad_pad[1, at, lanes]
                     grad_pad[0, at, lanes] = moved(value, -dilation)
                     grad_pad[2, at, lanes] = moved(value, dilation)
                 return carry
 
-            lax.fori_loop(0, side // 4, shift_step, 0)
+            lax.fori_loop(0, side // 8, shift_step, 0)
 
             def row_step(pair, sums):
                 sums = list(sums)
-                for extra in range(2):
-                    row = pair * 2 + extra
+                for extra in range(4):
+                    row = pair * 4 + extra
                     field = fields[span(base + row * side, side), lanes].astype(jnp.float32)
                     relu = jnp.maximum(field, 0.0)
                     back = jnp.zeros((side, LANES), jnp.float32)
@@ -214,7 +214,7 @@
                 return tuple(sums)
 
             start = tuple(taps_acc[j, 8 * t : 8 * t + 8, lanes] for t in range(9))
-            done = lax.fori_loop(0, side // 2, row_step, start)
+            done = lax.fori_loop(0, side // 4, row_step, start)
             for t in range(9):
                 taps_acc[j, 8 * t : 8 * t + 8, lanes] = done[t]
 

time: 182 us -> 179 us (0.984)
  Pallas kernels: 178 us -> 174 us
    pallas_call x1, Pallas kernels: 178 us -> 174 us  [local(): pl.pallas_call(functools.partial(kernel, micros, slots, sections, chips,...]
where the time goes in v3:
time: 179 us; the launch traced here: 178 us
  Pallas kernels  174 us (97%)
  local copies, waits for them, and re-layouts  3.33 us (2%)
    pallas_call x1, Pallas kernels, local(): pl.pallas_call(functools.partial(kernel, micros, slots, sections, chips,...  174 us

profile of v3, /device:TPU:0, one launch (start us, length us, event | category | flops | bytes accessed | tf_op | source)
XLA Modules:
  0.0 178.5 jit_solution(15523350052221266089)
XLA Ops:
  0.6 174.5 %shard_map.77 = (f32[4,64,512]{2,1,0:T(8,128)}, f32[64,128]{1,0:T(8,128)}) custom-call(s32[4]{0:T(128)} %labels.1, s32[4]{0:T(128)} %counts.1, bf16[4,16,16,512]{3,2,1,0:T(8,128)(2,1)} %images.1, bf16[9,4,512]{2,1,0:T(4,128)(2,1)} %bitcast.6, bf16[4,512,512]{2,1,0:T(8,128)(2,1)} %pointwise.1, f32[1000,512]{1,0:T(8,128)} %bitcast.4), custom_call_target="tpu_custom_call" | custom-call | tf_op jit(solution)/shard_map/pallas_call | solution.py:445
  175.1 0.8 constant_dynamic-slice_fusion
  176.0 0.6 copy.8
  176.6 1.9 %copy.10 = f32[4,64,512]{2,1,0:T(8,128)} copy(f32[4,64,512]{2,1,0:T(8,128)} %get-tuple-element.10) | data formatting | bytes 1048576
